TPU v7x, 128 devices: a whole 4x4x4 slice. The times are simulated.
128 devices in a mesh: gx: 16 (over z_lo, x, core), gy: 8 (over z_hi, y).
Axes of the slice: x: 4, y: 4, z: 4 (z_hi: 2, z_lo: 2; z = z_hi * 2 + z_lo), core: 2. Of those that a mesh axis runs over, the one named last changes fastest.
Arguments:
- directions: float32 [64, 6, 128, 1024], P(None, None, 'gx', 'gy'), may hold values from -6 to 6
- node_scale: float32 [128, 1024], P('gx', 'gy'), may hold values from 0.5 to 1.5
- boundary_mask: int32 [128, 1024], P('gx', 'gy'), may hold values 0 or 1
- stiffener_rows: int32 [8], replicated, may hold values from 0 to 127
- stiffener_cols: int32 [16], replicated, may hold values from 0 to 1023
- center_stiffness: float32 [6], replicated, may hold values from 3 to 6
- couplings: float32 [6, 6, 6], replicated, may hold values from -0.04 to 0.04
- stiffener_stiffness: float32 [2, 6], replicated, may hold values from 0.5 to 4
Outputs:
- basis: float32 [64, 6, 128, 1024], P(None, None, 'gx', 'gy')
- projected: float32 [64, 64], replicated
All inputs are finite; a program needn't handle non-finite values. No bound on the sum of `boundary_mask` on one device may be relied on, other than what follows from the above.
Results may differ from a plain program's by a relative error of at most 0.00016.
Values sent between devices are 32-bit elements; how exact they have to be, the bound alone decides.
A program may use at most 192 MiB of HBM per device.

v0:
```python
import functools
import math

import jax
import jax.numpy as jnp
import numpy as np
from jax import lax
from jax.experimental import pallas as pl
from jax.experimental.pallas import tpu as pltpu
from jax.sharding import PartitionSpec as P

MESH = pl.DeviceIdType.MESH
OFFSETS = ((1, 0), (0, 1), (1, 1), (1, -1), (2, 0), (0, 2))
F32 = jnp.float32
BF16 = jnp.bfloat16
COUNT, PARTS, ROWS, LANES = 64, 6, 8, 128
PIECES = 4
PANEL = 4
AHEAD = 2
GRAM_GROUP = 3
GROUPS = 4
PER = COUNT // GROUPS
BATCH = 8
STEPS = (-1, 0, 1, 2)
NODE_ROWS = PARTS * ROWS


def halo_row(step_y, x):
    return {0: {8: 0, 9: 1, -2: 6, -1: 7}, 1: {8: 3, -1: 2}, -1: {8: 5, -1: 4}}[step_y][x]


DEPTH = (len(STEPS) + 1) * NODE_ROWS


def stencil_masks():
    n = len(OFFSETS)
    out = np.zeros((2 * n, ROWS, DEPTH), np.float32)
    for i, sign in enumerate((1, -1)):
        for q, (ox, oy) in enumerate(OFFSETS):
            dx, dy = sign * ox, sign * oy
            for x in range(ROWS):
                for d in range(PARTS):
                    if dy not in STEPS:
                        continue
                    if 0 <= x + dx < ROWS:
                        at = STEPS.index(dy) * NODE_ROWS + d * ROWS + x + dx
                    else:
                        at = len(STEPS) * NODE_ROWS + d * ROWS + halo_row(dy, x + dx)
                    out[i * n + q, x, at] = 1.0
    return out


def spread():
    out = np.zeros((PARTS, DEPTH), np.float32)
    for at in range(DEPTH):
        out[(at % NODE_ROWS) // ROWS, at] = 1.0
    return out


def split(x):
    hi = x.astype(BF16)
    return hi, (x - hi.astype(F32)).astype(BF16)


def build(coup_ref, spread_ref, mask_ref, both, out_ref):
    n = len(OFFSETS)
    expand = spread_ref[...]
    rows, beside = [None] * PARTS, []
    for s in range(2 * n - 1 if both else n):
        dims = (((1 if s < n else 0,), (0,)), ((), ()))
        wide = lax.dot_general(
            coup_ref[s % n], expand, dims, precision=lax.Precision.HIGHEST, preferred_element_type=F32
        )
        for c in range(PARTS):
            term = wide[c : c + 1, :] * mask_ref[s]
            rows[c] = term if rows[c] is None else rows[c] + term
    near = mask_ref[0] + mask_ref[n] if both else mask_ref[0]
    for c in range(PARTS):
        beside.append(expand[c : c + 1, :] * near)
    hi, lo = split(jnp.concatenate(rows, axis=0))
    out_ref[0:NODE_ROWS] = hi
    out_ref[NODE_ROWS : 2 * NODE_ROWS] = jnp.concatenate(beside, axis=0).astype(BF16)
    out_ref[2 * NODE_ROWS :] = lo


def stencil_kernel(
    gx, gy,
    dir_hbm, scale_hbm, mask_hbm, srow_hbm, scol_hbm, center_hbm, coup_hbm, stiff_hbm,
    masks_hbm, spread_hbm,
    basis_out, projected_ref,
    dir_ref, scale_ref, mask_ref, srow_ref, scol_ref, center_ref, coup_ref, stiff_ref,
    masks_ref, spread_ref, in_sems, dir_sems,
    u, hx, prod, u2, hx2, image,
    pk, pyp, pym, hcp, hcm, pk2, py2p, py2m, hc2p, hc2m,
    m1, m2, far_coup, flat, iflat, g_own, g_a, g_b, c_own, c_a, c_b, basis,
    xs_send, xs_recv, ys_send, ys_recv, cs_send, cs_recv,
    ga_send, ga_recv, gb_send, gb_recv, ca_send, ca_recv, cb_send, cb_recv, out_sem,
):
    small = [
        pltpu.make_async_copy(src, dst, in_sems.at[i])
        for i, (src, dst) in enumerate((
            (scale_hbm, scale_ref), (mask_hbm, mask_ref), (srow_hbm, srow_ref), (scol_hbm, scol_ref),
            (center_hbm, center_ref), (coup_hbm, coup_ref), (stiff_hbm, stiff_ref), (masks_hbm, masks_ref),
            (spread_hbm, spread_ref),
        ))
    ]
    large = []
    for i in range(GROUPS):
        part = pl.ds(i * PER * PARTS, PER * PARTS)
        large.append(pltpu.make_async_copy(dir_hbm.at[part], dir_ref.at[part], dir_sems.at[i]))
    for copy in small[:2] + large + small[2:]:
        copy.start()
    ix, iy = lax.axis_index("gx"), lax.axis_index("gy")
    xp, xm = lax.rem(ix + 1, gx), lax.rem(ix + gx - 1, gx)
    yp, ym = lax.rem(iy + 1, gy), lax.rem(iy + gy - 1, gy)

    barrier = pltpu.get_barrier_semaphore()

    def greet(px, py):
        pl.semaphore_signal(barrier, inc=1, device_id=(px, py), device_id_type=MESH)

    na, nb = gx // 2, 2 * gy
    ia, ib = lax.rem(ix, na), lax.div(ix, na) * gy + iy

    def peer_a(j):
        return lax.div(ix, na) * na + lax.rem(ia + j, na), iy

    def peer_b(j):
        to = lax.rem(ib + j, nb)
        return lax.div(to, gy) * na + ia, lax.rem(to, gy)

    for j in range(1, na):
        greet(*peer_a(j))
    for j in range(1, nb):
        greet(*peer_b(j))
    for px in (xp, xm):
        greet(px, iy)
        for py in (yp, ym):
            greet(px, py)
    for py in (yp, ym):
        greet(ix, py)

    lane = lax.broadcasted_iota(jnp.int32, (ROWS, LANES), 1)
    row = lax.broadcasted_iota(jnp.int32, (ROWS, LANES), 0)
    small[0].wait()
    small[1].wait()
    mask = mask_ref[...].astype(F32)
    weight = scale_ref[...] * (1.0 - mask)

    def scale_body(i, _):
        g = lax.div(i, PER // BATCH)
        m = lax.rem(i, PER // BATCH) * BATCH
        for c in range(PARTS):
            packed = pk[g * PARTS + c]
            for b in range(BATCH):
                at = (i * BATCH + b) * PARTS + c
                value = weight * dir_ref[at]
                u[at] = value
                moved = pltpu.roll(value, lax.rem(4 * (m + b) + 2, LANES), 1)
                packed = jnp.where(lax.div(lane, 4) == m + b, moved, packed)
            pk[g * PARTS + c] = packed
        return 0

    pk[...] = jnp.zeros_like(pk)

    def remote(src, dst, send, recv, px, py):
        return pltpu.make_async_remote_copy(
            src_ref=src, dst_ref=dst, send_sem=send, recv_sem=recv,
            device_id=(px, py), device_id_type=MESH,
        )

    def x_copies(src, dst, g, base, down):
        part = pl.ds(g * PER * PARTS, PER * PARTS)
        top = pl.ds(0, 2)
        out = [remote(src.at[part, top], dst.at[part, top], xs_send.at[base], xs_recv.at[base], xm, iy)]
        if down:
            low = pl.ds(6, 2)
            out.append(
                remote(src.at[part, low], dst.at[part, low], xs_send.at[base + 1], xs_recv.at[base + 1], xp, iy)
            )
        return out

    def y_copies(src, dst_p, dst_m, cp, cm, part, base, down):
        first = pl.ds(0, 1)
        last = pl.ds(7, 1)
        out = [
            remote(src.at[part], dst_p.at[part], ys_send.at[base], ys_recv.at[base], ix, ym),
            remote(src.at[part], dst_m.at[part], ys_send.at[base + 1], ys_recv.at[base + 1], ix, yp),
        ]
        k = 2 * base
        out.append(remote(src.at[part, first], cp.at[part, first], cs_send.at[k], cs_recv.at[k], xm, ym))
        out.append(remote(src.at[part, first], cm.at[part, first], cs_send.at[k + 1], cs_recv.at[k + 1], xm, yp))
        if down:
            out.append(remote(src.at[part, last], cp.at[part, last], cs_send.at[k + 2], cs_recv.at[k + 2], xp, ym))
            out.append(remote(src.at[part, last], cm.at[part, last], cs_send.at[k + 3], cs_recv.at[k + 3], xp, yp))
        return out

    firsts = []
    for g in range(GROUPS):
        large[g].wait()
        lax.fori_loop(g * PER // BATCH, (g + 1) * PER // BATCH, scale_body, 0)
        if g == 0:
            pl.semaphore_wait(barrier, (na - 1) + (nb - 1) + 8)
        copies = y_copies(pk, pyp, pym, hcp, hcm, pl.ds(g * PARTS, PARTS), 2 * g, True)
        copies += x_copies(u, hx, g, 2 * g, True)
        if g >= AHEAD:
            for copy in firsts[g - AHEAD]:
                copy.wait_send()
        for copy in copies:
            copy.start()
        firsts.append(copies)

    for copy in small[2:]:
        copy.wait()

    rows_hit = jnp.zeros((ROWS, LANES), F32)
    for f in range(srow_ref.shape[0]):
        rows_hit = rows_hit + (row + ix * ROWS == srow_ref[f]).astype(F32)
    cols_hit = jnp.zeros((ROWS, LANES), F32)
    for f in range(scol_ref.shape[0]):
        cols_hit = cols_hit + (lane + iy * LANES == scol_ref[f]).astype(F32)
    build(coup_ref, spread_ref, masks_ref, True, m1)
    build(coup_ref, spread_ref, masks_ref, False, m2)
    last = coup_ref[len(OFFSETS) - 1]
    for c in range(PARTS):
        for d in range(PARTS):
            far_coup[c * PARTS + d] = jnp.broadcast_to(last[d : d + 1, c : c + 1], (ROWS, LANES))

    zero = jnp.zeros((ROWS, LANES), F32)
    from_minus = lax.rem(lane, 4) < 2
    in_xp = jnp.full((ROWS, LANES), ix, jnp.int32) < gx - 1
    in_xm = jnp.full((ROWS, LANES), ix, jnp.int32) > 0
    in_yp = jnp.full((ROWS, LANES), iy, jnp.int32) < gy - 1
    in_ym = jnp.full((ROWS, LANES), iy, jnp.int32) > 0
    in_x = (in_xp & (row < 4)) | (in_xm & (row >= 4))
    in_x2 = in_xp & (row < 2)
    in_y = (in_ym & from_minus) | (in_yp & (lax.rem(lane, 4) >= 2))

    def merge_y(minus, plus, cminus, cplus, n, start, in_corner):
        for i in range(n):
            at = start + i
            plus[at] = jnp.where(in_y, jnp.where(from_minus, minus[at], plus[at]), zero)
            cplus[at] = jnp.where(in_y & in_corner, jnp.where(from_minus, cminus[at], cplus[at]), zero)

    def windows(source, hx_ref, py_ref, hc_ref, k, g, m, inside, both):
        back = LANES - 2 - 4 * m
        tiles = {s: [] for s in STEPS}
        halo, far = [], []
        for d in range(PARTS):
            at = k * PARTS + d
            v = source[at]
            h = jnp.where(inside, hx_ref[at], zero)
            hy = pltpu.roll(py_ref[g * PARTS + d], back, 1)
            hc = pltpu.roll(hc_ref[g * PARTS + d], back, 1)
            for s in STEPS:
                if s == 0:
                    tiles[s].append(v)
                elif s > 0:
                    tiles[s].append(pltpu.roll(jnp.where(lane < s, hy, v), LANES - s, 1))
                else:
                    tiles[s].append(pltpu.roll(jnp.where(lane >= LANES + s, hy, v), -s, 1))
            if both:
                far.append(pltpu.roll(jnp.where(lane >= LANES - 2, hy, v), 2, 1))
            right = pltpu.roll(jnp.where(lane < 1, hc, h), LANES - 1, 1)
            left = pltpu.roll(jnp.where(lane >= LANES - 1, hc, h), 1, 1)
            right = pltpu.roll(right, 3, 0)
            left = pltpu.roll(left, 5, 0)
            halo.append(jnp.where((row == 2) | (row == 3), right, jnp.where((row == 4) | (row == 5), left, h)))
        stack = jnp.concatenate([t for s in STEPS for t in tiles[s]] + halo, axis=0)
        return stack, tiles, far

    def couple(stacks, m_ref):
        hi, lo = split(jnp.concatenate(stacks, axis=1))
        top = jnp.dot(m_ref[...], hi, preferred_element_type=F32)
        low = jnp.dot(m_ref[0 : 2 * NODE_ROWS], lo, preferred_element_type=F32)
        return top[0:NODE_ROWS] + (top[2 * NODE_ROWS :] + low[0:NODE_ROWS]), (
            top[NODE_ROWS : 2 * NODE_ROWS] + low[NODE_ROWS:]
        )

    def tile_of(x, c, b):
        return x[c * ROWS : (c + 1) * ROWS, b * LANES : (b + 1) * LANES]

    def apply_body(g, i, _):
        m = i * BATCH
        first = g * PER + m
        got = [windows(u, hx, pyp, hcp, first + b, g, m + b, in_x, True) for b in range(BATCH)]
        total, beside = couple([w[0] for w in got], m1)
        for c in range(PARTS):
            packed = pk2[g * PARTS + c]
            frame = stiff_ref[0, c] * rows_hit
            stringer = stiff_ref[1, c] * cols_hit
            local = center_ref[c] + 2.0 * frame + 2.0 * stringer
            for b in range(BATCH):
                _, tiles, far = got[b]
                v = tile_of(total, c, b) + local * tiles[0][c]
                v = v - frame * (tiles[1][c] + tiles[-1][c]) - stringer * tile_of(beside, c, b)
                for d in range(PARTS):
                    v = v + far_coup[c * PARTS + d] * far[d]
                at = (first + b) * PARTS + c
                value = weight * v + mask * dir_ref[at]
                prod[pl.ds(pl.multiple_of(at * ROWS, ROWS), ROWS), :] = value
                scaled = weight * value
                u2[at] = scaled
                moved = pltpu.roll(scaled, lax.rem(4 * (m + b) + 2, LANES), 1)
                packed = jnp.where(lax.div(lane, 4) == m + b, moved, packed)
            pk2[g * PARTS + c] = packed
        return 0

    pk2[...] = jnp.zeros_like(pk2)
    second = []
    for g in range(GROUPS):
        for copy in firsts[g]:
            copy.wait_recv()
        merge_y(pym, pyp, hcm, hcp, PARTS, g * PARTS, in_x)
        lax.fori_loop(0, PER // BATCH, functools.partial(apply_body, g), 0)
        x2 = x_copies(u2, hx2, g, 2 * GROUPS + g, False)
        y2 = y_copies(pk2, py2p, py2m, hc2p, hc2m, pl.ds(g * PARTS, PARTS), 2 * GROUPS + 2 * g, False)
        for copy in y2 + x2:
            copy.start()
        second.append(y2 + x2)

    def send_all(own, slots, mine, peer, count, send, recv):
        copies = []
        for j in range(1, count):
            copies.append(remote(own, slots.at[mine], send.at[j], recv.at[j], *peer(j)))
        for copy in copies:
            copy.start()
        return copies

    def receive_sum(copies, own, slots, mine, count):
        slots[mine] = own[...]
        for copy in copies:
            copy.wait_recv()
        total = slots[0]
        for j in range(1, count):
            total = total + slots[j]
        return total

    def regroup(source, target):
        for at in range(NODE_ROWS):
            hi, lo = split(source[pl.ds(at, COUNT, stride=NODE_ROWS), :])
            target[0:COUNT, at * LANES : (at + 1) * LANES] = hi
            target[COUNT : 2 * COUNT, at * LANES : (at + 1) * LANES] = lo

    def inner(left, right):
        big = lax.dot_general(left[...], right[...], (((1,), (1,)), ((), ())), preferred_element_type=F32)
        fold = big[0:COUNT] + big[COUNT : 2 * COUNT]
        fold = fold[:, 0:COUNT] + fold[:, COUNT : 2 * COUNT]
        return jnp.concatenate([fold[0 : COUNT // 2], fold[COUNT // 2 :]], axis=1)

    def unfold(x):
        return jnp.concatenate([x[:, 0:COUNT], x[:, COUNT : 2 * COUNT]], axis=0)

    regroup(prod, flat)
    g_own[0] = inner(flat, flat)
    g_first = send_all(g_own.at[0], g_a, ia, peer_a, na, ga_send, ga_recv)

    def image_body(g, i, _):
        m = i * BATCH
        first = g * PER + m
        got = [windows(u2, hx2, py2p, hc2p, first + b, g, m + b, in_x2, False) for b in range(BATCH)]
        total, beside = couple([w[0] for w in got], m2)
        for c in range(PARTS):
            frame = stiff_ref[0, c] * rows_hit
            stringer = stiff_ref[1, c] * cols_hit
            local = 0.5 * center_ref[c] + frame + stringer
            for b in range(BATCH):
                _, tiles, _ = got[b]
                v = tile_of(total, c, b) + local * tiles[0][c]
                v = v - frame * tiles[1][c] - stringer * tile_of(beside, c, b)
                at = pl.ds(pl.multiple_of(((first + b) * PARTS + c) * ROWS, ROWS), ROWS)
                image[at, :] = weight * v + (0.5 * mask) * prod[at, :]
        return 0

    for g in range(GROUPS):
        for copy in second[g]:
            copy.wait_recv()
        merge_y(py2m, py2p, hc2m, hc2p, PARTS, g * PARTS, in_x2)
        lax.fori_loop(0, PER // BATCH, functools.partial(image_body, g), 0)
        if g == GRAM_GROUP:
            g_own[1] = receive_sum(g_first, g_own.at[0], g_a, ia, na)
            g_second = send_all(g_own.at[1], g_b, ib, peer_b, nb, gb_send, gb_recv)
    regroup(image, iflat)
    c_own[0] = inner(flat, iflat)
    c_first = send_all(c_own.at[0], c_a, ia, peer_a, na, ca_send, ca_recv)

    c_own[1] = receive_sum(c_first, c_own.at[0], c_a, ia, na)
    c_second = send_all(c_own.at[1], c_b, ib, peer_b, nb, cb_send, cb_recv)
    gram = unfold(receive_sum(g_second, g_own.at[1], g_b, ib, nb))
    tiles = []
    for i in range(COUNT // ROWS):
        unit = (lax.broadcasted_iota(jnp.int32, (ROWS, COUNT), 1) == i * ROWS
                + lax.broadcasted_iota(jnp.int32, (ROWS, COUNT), 0)).astype(F32)
        tiles.append(jnp.concatenate([gram[i * ROWS : (i + 1) * ROWS], unit], axis=1))
    for first in range(0, COUNT, PANEL):
        block, inside = first // ROWS, first % ROWS
        here = range(block, COUNT // ROWS)
        cols = [{i: jnp.broadcast_to(tiles[i][:, first + j : first + j + 1], (ROWS, LANES)) for i in here}
                for j in range(PANEL)]
        lines = [tiles[block][inside + j : inside + j + 1, :] for j in range(PANEL)]
        for a in range(PANEL):
            at = inside + a
            over = 1.0 / cols[a][block][at : at + 1, :]
            line = lines[a] * over
            for j in range(a + 1, PANEL):
                ratio = cols[j][block][at : at + 1, :] * over
                lines[j] = lines[j] - cols[a][block][inside + j : inside + j + 1, :] * line
                for i in here:
                    cols[j][i] = cols[j][i] - cols[a][i] * ratio
            for i in here:
                col = jnp.where(row > at, cols[a][i], 0.0) if i == block else cols[a][i]
                tiles[i] = tiles[i] - col * line
    for i in range(COUNT // ROWS):
        pivots = jnp.sum(jnp.where(lane == row + i * ROWS, tiles[i], 0.0), axis=1, keepdims=True)
        tiles[i] = tiles[i] * lax.rsqrt(pivots)
    inverse_t = jnp.concatenate(tiles, axis=0)[:, COUNT : 2 * COUNT]

    scale = math.sqrt(PARTS * gx * ROWS * gy * LANES)
    hi, lo = split(scale * inverse_t)
    factors = jnp.concatenate([hi, hi, lo], axis=1)
    width = 2 * LANES
    for i in range(NODE_ROWS // 2):
        cols = slice(i * width, (i + 1) * width)
        fields = jnp.concatenate([flat[:, cols], flat[0:COUNT, cols]], axis=0)
        value = jnp.dot(factors, fields, preferred_element_type=F32)
        for j in range(2):
            basis[pl.ds(2 * i + j, COUNT, stride=NODE_ROWS), :] = value[:, j * LANES : (j + 1) * LANES]
    keep = pltpu.make_async_copy(basis, basis_out, out_sem)
    keep.start()

    half = unfold(receive_sum(c_second, c_own.at[1], c_b, ib, nb))
    cross = half + half.T
    left = jnp.dot(inverse_t, cross, precision=lax.Precision.HIGHEST, preferred_element_type=F32)
    projected_ref[...] = lax.dot_general(
        left, inverse_t, (((1,), (1,)), ((), ())), precision=lax.Precision.HIGHEST, preferred_element_type=F32
    )
    for copy in [c for g in firsts[-AHEAD:] + second for c in g]:
        copy.wait_send()
    for copy in g_first + g_second + c_first + c_second:
        copy.wait_send()
    keep.wait()


def hand_over_kernel(basis_in, projected_in, basis_out, projected_out, basis, projected, in_sems, out_sems):
    rows = basis_in.shape[0] // PIECES
    ways = [(basis_in.at[part], basis.at[part], basis_out.at[part])
            for part in (pl.ds(i * rows, rows) for i in range(PIECES))]
    ways.append((projected_in, projected, projected_out))
    arrive = [pltpu.make_async_copy(a, b, in_sems.at[i]) for i, (a, b, _) in enumerate(ways)]
    leave = [pltpu.make_async_copy(b, c, out_sems.at[i]) for i, (_, b, c) in enumerate(ways)]
    for copy in arrive:
        copy.start()
    for first, then in zip(arrive, leave):
        first.wait()
        then.start()
    for copy in leave:
        copy.wait()


def body(gx, gy, directions, node_scale, boundary_mask, stiffener_rows, stiffener_cols, center, couplings, stiffness):
    tiles = COUNT * PARTS
    nodes = NODE_ROWS * LANES
    na, nb = gx // 2, 2 * gy
    vmem = pl.BlockSpec(memory_space=pltpu.VMEM)
    hbm = pl.BlockSpec(memory_space=pl.ANY)
    field = pltpu.VMEM((tiles, ROWS, LANES), F32)
    plain = pltpu.VMEM((tiles * ROWS, LANES), F32)
    edge = pltpu.VMEM((GROUPS * PARTS, ROWS, LANES), F32)
    parts = pltpu.VMEM((2 * COUNT, nodes), BF16)
    matrix = pltpu.VMEM((3 * NODE_ROWS, DEPTH), BF16)
    small = (COUNT // 2, 2 * COUNT)
    dma = pltpu.SemaphoreType.DMA
    basis, projected = pl.pallas_call(
        functools.partial(stencil_kernel, gx, gy),
        out_shape=(
            jax.ShapeDtypeStruct((tiles * ROWS, LANES), F32),
            jax.ShapeDtypeStruct((COUNT, COUNT), F32),
        ),
        in_specs=[hbm] * 10,
        out_specs=(hbm, vmem),
        scratch_shapes=[
            field, pltpu.VMEM((ROWS, LANES), F32), pltpu.VMEM((ROWS, LANES), jnp.int32),
            pltpu.SMEM(stiffener_rows.shape, jnp.int32), pltpu.SMEM(stiffener_cols.shape, jnp.int32),
            pltpu.SMEM((PARTS,), F32), pltpu.VMEM((len(OFFSETS), PARTS, PARTS), F32), pltpu.SMEM((2, PARTS), F32),
            pltpu.VMEM((2 * len(OFFSETS), ROWS, DEPTH), F32), pltpu.VMEM((PARTS, DEPTH), F32),
            dma((9,)), dma((GROUPS,)),
            field, field, plain, field, field, plain,
            edge, edge, edge, edge, edge, edge, edge, edge, edge, edge,
            matrix, matrix, pltpu.VMEM((PARTS * PARTS, ROWS, LANES), F32), parts, parts,
            pltpu.VMEM((2,) + small, F32), pltpu.VMEM((na,) + small, F32), pltpu.VMEM((nb,) + small, F32),
            pltpu.VMEM((2,) + small, F32), pltpu.VMEM((na,) + small, F32), pltpu.VMEM((nb,) + small, F32),
            plain,
            dma((3 * GROUPS,)), dma((3 * GROUPS,)),
            dma((4 * GROUPS,)), dma((4 * GROUPS,)),
            dma((8 * GROUPS,)), dma((8 * GROUPS,)),
            dma((na,)), dma((na,)), dma((nb,)), dma((nb,)),
            dma((na,)), dma((na,)), dma((nb,)), dma((nb,)),
            dma(()),
        ],
        compiler_params=pltpu.CompilerParams(
            collective_id=0, has_side_effects=True, vmem_limit_bytes=63 * 1024 * 1024
        ),
        name="stencil",
    )(
        directions.reshape(tiles, ROWS, LANES), node_scale, boundary_mask, stiffener_rows, stiffener_cols,
        center, couplings, stiffness, jnp.asarray(stencil_masks()), jnp.asarray(spread()),
    )
    basis, projected = pl.pallas_call(
        hand_over_kernel,
        out_shape=(
            jax.ShapeDtypeStruct((tiles * ROWS, LANES), F32),
            jax.ShapeDtypeStruct((COUNT, COUNT), F32),
        ),
        in_specs=[hbm, hbm],
        out_specs=(hbm, hbm),
        scratch_shapes=[plain, pltpu.VMEM((COUNT, COUNT), F32), dma((PIECES + 1,)), dma((PIECES + 1,))],
        compiler_params=pltpu.CompilerParams(vmem_limit_bytes=63 * 1024 * 1024),
        name="hand_over",
    )(basis, projected)
    return basis.reshape(COUNT, PARTS, ROWS, LANES), projected


def solution(mesh):
    gx, gy = mesh.shape["gx"], mesh.shape["gy"]
    in_specs = (P(None, None, "gx", "gy"), P("gx", "gy"), P("gx", "gy"), P(), P(), P(), P(), P())
    out_specs = (P(None, None, "gx", "gy"), P())
    return jax.shard_map(
        functools.partial(body, gx, gy), mesh=mesh, in_specs=in_specs, out_specs=out_specs, check_vma=False
    )
```

profile of v0, /device:TPU:1, one launch (start us, length us, event | category | flops | bytes accessed | tf_op | source)
XLA Modules:
  0.0 45.3 jit_solution(5465672876472551989)
XLA Ops:
  0.6 42.4 %stencil.1 = (f32[3072,128]{1,0:T(8,128)}, f32[64,64]{1,0:T(8,128)}) custom-call(f32[384,8,128]{2,1,0:T(8,128)} %bitcast.2, f32[8,128]{1,0:T(8,128)} %scale_hbm.1, s32[8,128]{1,0:T(8,128)} %mask_hbm.1, s32[8]{0:T(128)} %srow_hbm.1, s32[16]{0:T(128)} %scol_hbm.1, f32[6]{0:T(128)} %center_hbm.1, f32[6,6,6]{2,1,0:T(8,128)} %coup_hbm.1, f32[2,6]{1,0:T(2,128)} %stiff_hbm.1, ...), custom_call_target="tpu_custom_call" | custom-call | tf_op jit(solution)/shard_map/stencil/pallas_call | solution.py:473
  43.1 2.2 %hand_over.1 = (f32[3072,128]{1,0:T(8,128)}, f32[64,64]{1,0:T(8,128)}) custom-call(f32[3072,128]{1,0:T(8,128)} %get-tuple-element.6.basis_in, f32[64,64]{1,0:T(8,128)} %get-tuple-element.7.projected_in), custom_call_target="tpu_custom_call" | custom-call | tf_op jit(solution)/shard_map/hand_over/pallas_call | solution.py:508
where the time goes:
time: 45.4 us; the launch traced here: 45.3 us
  Pallas kernels  44.6 us (98%)
  between operations  0.64 us (1%)
    pallas_call x1, Pallas kernels, body(): pl.pallas_call(functools.partial(stencil_kernel, gx, gy), out_shape=(jax....  42.4 us
    pallas_call x1, Pallas kernels, body(): pl.pallas_call(hand_over_kernel, out_shape=(jax.ShapeDtypeStruct((tiles *...  2.22 us

commit v1 on v0

--- a/solution.py
+++ b/solution.py
@@ -206,7 +206,7 @@
         if g >= AHEAD:
             for copy in firsts[g - AHEAD]:
                 copy.wait_send()
-        for copy in copies:
+        for copy in copies[2:] + copies[:2]:
             copy.start()
         firsts.append(copies)
 
@@ -315,7 +315,7 @@
         lax.fori_loop(0, PER // BATCH, functools.partial(apply_body, g), 0)
         x2 = x_copies(u2, hx2, g, 2 * GROUPS + g, False)
         y2 = y_copies(pk2, py2p, py2m, hc2p, hc2m, pl.ds(g * PARTS, PARTS), 2 * GROUPS + 2 * g, False)
-        for copy in y2 + x2:
+        for copy in y2[2:] + x2 + y2[:2]:
             copy.start()
         second.append(y2 + x2)
 

time: 45.4 us -> 45.4 us (level)
  no operation moved by 1% of the time
where the time goes in v1:
time: 45.4 us; the launch traced here: 45.3 us
  Pallas kernels  44.7 us (98%)
  between operations  0.64 us (1%)
    pallas_call x1, Pallas kernels, body(): pl.pallas_call(functools.partial(stencil_kernel, gx, gy), out_shape=(jax....  42.4 us
    pallas_call x1, Pallas kernels, body(): pl.pallas_call(hand_over_kernel, out_shape=(jax.ShapeDtypeStruct((tiles *...  2.22 us

profile of v1, /device:TPU:1, one launch (start us, length us, event | category | flops | bytes accessed | tf_op | source)
XLA Modules:
  0.0 45.3 jit_solution(7915271565728561167)
XLA Ops:
  0.6 42.4 %stencil.1 = (f32[3072,128]{1,0:T(8,128)}, f32[64,64]{1,0:T(8,128)}) custom-call(f32[384,8,128]{2,1,0:T(8,128)} %bitcast.2, f32[8,128]{1,0:T(8,128)} %scale_hbm.1, s32[8,128]{1,0:T(8,128)} %mask_hbm.1, s32[8]{0:T(128)} %srow_hbm.1, s32[16]{0:T(128)} %scol_hbm.1, f32[6]{0:T(128)} %center_hbm.1, f32[6,6,6]{2,1,0:T(8,128)} %coup_hbm.1, f32[2,6]{1,0:T(2,128)} %stiff_hbm.1, ...), custom_call_target="tpu_custom_call" | custom-call | tf_op jit(solution)/shard_map/stencil/pallas_call | solution.py:473
  43.1 2.2 %hand_over.1 = (f32[3072,128]{1,0:T(8,128)}, f32[64,64]{1,0:T(8,128)}) custom-call(f32[3072,128]{1,0:T(8,128)} %get-tuple-element.6.basis_in, f32[64,64]{1,0:T(8,128)} %get-tuple-element.7.projected_in), custom_call_target="tpu_custom_call" | custom-call | tf_op jit(solution)/shard_map/hand_over/pallas_call | solution.py:508
